TPU v7x, 1024 devices: a whole 8x8x8 slice. The times are simulated.
1024 devices in a mesh: tensor: 8 (over z_hi, core), replica: 16 (over x, z_lo), fsdp: 8 (over y).
Axes of the slice: x: 8, y: 8, z: 8 (z_hi: 4, z_lo: 2; z = z_hi * 2 + z_lo), core: 2. Of those that a mesh axis runs over, the one named last changes fastest.
Arguments:
- gradients: bfloat16 [16, 2048, 28672], P('replica', 'fsdp', 'tensor'), may hold values from -6 to 6
- seeds: int32 [2], replicated, may hold values from 0 to 1073741823
- adam_step: int32 [1], replicated, may hold values from 1 to 8
- first_moment: float32 [2048, 28672], P(('fsdp', 'replica'), 'tensor'), may hold values from -0.6 to 0.6
- second_moment: float32 [2048, 28672], P(('fsdp', 'replica'), 'tensor'), may hold values from 0.001 to 0.1
Outputs:
- new_first: float32 [2048, 28672], P(('fsdp', 'replica'), 'tensor')
- new_second: float32 [2048, 28672], P(('fsdp', 'replica'), 'tensor')
- step_update: float32 [2048, 28672], P(('fsdp', 'replica'), 'tensor')
All inputs are finite; a program needn't handle non-finite values.
Results may differ from a plain program's by a relative error of at most 0.012.
The roundings to bfloat16 on the way count: a program that leaves them out, or rounds other values in their place, can miss the bound.
Values may be sent and summed in bfloat16 or wider, within the bound.
A program may use at most 32 MiB of HBM per device.

v0:
```python
import math

import jax
import jax.numpy as jnp
from jax import lax
from jax.sharding import PartitionSpec as P

RANK = 512


def scramble(value):
    value = value ^ lax.shift_right_logical(value, jnp.full_like(value, 16))
    value = value * jnp.int32(-2048144789)
    value = value ^ lax.shift_right_logical(value, jnp.full_like(value, 13))
    value = value * jnp.int32(-1028477387)
    value = value ^ lax.shift_right_logical(value, jnp.full_like(value, 16))
    return value


def projection_block(first_column, columns, rank, seeds):
    seed_key = seeds[0] ^ seeds[1] * jnp.int32(668265263)
    column = lax.broadcasted_iota(jnp.int32, (columns, rank), 0) + first_column
    entry = lax.broadcasted_iota(jnp.int32, (columns, rank), 1)
    counter = (column * jnp.int32(rank) + entry) * jnp.int32(2)
    hash_a = scramble(counter * jnp.int32(-1640531535) ^ seed_key)
    hash_b = scramble((counter + jnp.int32(1)) * jnp.int32(-1640531535) ^ seed_key)
    inverse = 1.0 / 16777216.0
    uniform_a = (
        lax.shift_right_logical(hash_a, jnp.full_like(hash_a, 8)).astype(jnp.float32) + 0.5
    ) * inverse
    uniform_b = (
        lax.shift_right_logical(hash_b, jnp.full_like(hash_b, 8)).astype(jnp.float32) + 0.5
    ) * inverse
    gauss = jnp.sqrt(-2.0 * jnp.log(uniform_a)) * jnp.cos(6.283185307179586 * uniform_b)
    return (gauss * rank ** (-0.5)).astype(jnp.bfloat16)


def per_device(gradients, seeds, adam_step, first_moment, second_moment):
    gradient = gradients[0]
    columns = gradient.shape[1]
    replicas = lax.axis_size("replica")
    column_start = lax.axis_index("tensor") * jnp.int32(columns)
    piece_cols = math.gcd(columns, 512)
    blocks = columns // piece_cols
    starts = column_start + lax.iota(jnp.int32, blocks) * jnp.int32(piece_cols)
    tiles = lax.map(lambda first: projection_block(first, piece_cols, RANK, seeds), starts)
    projection = tiles.reshape(columns, RANK)
    partial_value = jnp.dot(gradient, projection, preferred_element_type=jnp.float32) * (
        1.0 / replicas
    )
    share = lax.psum_scatter(partial_value, "replica", scatter_dimension=0, tiled=True)
    sketch = lax.psum(share, "tensor")
    sketch_rounded = sketch.astype(jnp.bfloat16)
    estimate = lax.dot_general(
        sketch_rounded, projection, (((1,), (1,)), ((), ())), preferred_element_type=jnp.float32
    )
    new_first = 0.9 * first_moment + 0.1 * estimate
    new_second = 0.95 * second_moment + 0.05 * estimate * estimate
    step_float = adam_step[0].astype(jnp.float32)
    fix_first = 1.0 - jnp.power(jnp.float32(0.9), step_float)
    fix_second = 1.0 - jnp.power(jnp.float32(0.95), step_float)
    step_update = new_first / fix_first / (jnp.sqrt(new_second / fix_second) + 1e-08)
    return (new_first, new_second, step_update)


def solution(mesh):
    placed = (
        P("replica", "fsdp", "tensor"),
        P(),
        P(),
        P(("fsdp", "replica"), "tensor"),
        P(("fsdp", "replica"), "tensor"),
    )
    return jax.shard_map(
        per_device,
        mesh=mesh,
        in_specs=placed,
        out_specs=(
            P(("fsdp", "replica"), "tensor"),
            P(("fsdp", "replica"), "tensor"),
            P(("fsdp", "replica"), "tensor"),
        ),
        check_vma=False,
    )
```

profile of v0, /device:TPU:1, one launch (start us, length us, event | category | flops | bytes accessed | tf_op | source)
XLA Modules:
  0.0 192.2 jit_solution(13961427840035636405)
XLA Ops:
  7.2 0.0 copy-start
  7.2 0.0 reduce-scatter.4.cloned.1.call-start
  7.2 1.4 fusion.32
  9.9 49.7 %while.12 = (s32[]{:T(128)}, bf16[7,512,512]{2,1,0:T(8,128)(2,1)}, s32[7]{0:T(128)S(1)}, s32[]{:T(128)}, s32[]{:T(128)}) while((s32[]{:T(128)}, bf16[7,512,512]{2,1,0:T(8,128)(2,1)}, s32[7]{0:T(128)S(1)}, s32[]{:T(128)}, s32[]{:T(128)}) %tuple.33), condition=%wide.region_1.2_spmd, body=%wide.region_0.1_spmd.sunk | while | flops 9176066 | bytes 529485 | solution.py:46
  9.9 0.6 dynamic_slice.8
  10.5 0.6 add_multiply_fusion.2
  11.2 5.9 %fusion.37 = bf16[7,512,512]{2,1,0:T(8,128)(2,1)} fusion(bf16[7,512,512]{2,1,0:T(8,128)(2,1)} %get-tuple-element.105, s32[]{:T(128)} %get-tuple-element.104, s32[]{:T(128)} %get-tuple-element.112, s32[512]{0:T(512)S(1)} %add_multiply_fusion.2), kind=kLoop, calls=%fused_computation.25.clone.1 | loop fusion | flops 9175040 | bytes 527360 | tf_op jit(solution)/shard_map/while/body/jit(dynamic_update_index_in_dim)/dynamic_update_slice | solution.py:46
  17.0 0.6 dynamic_slice.8
  17.6 0.6 add_multiply_fusion.2
  18.3 5.9 %fusion.37 = bf16[7,512,512]{2,1,0:T(8,128)(2,1)} fusion(bf16[7,512,512]{2,1,0:T(8,128)(2,1)} %get-tuple-element.105, s32[]{:T(128)} %get-tuple-element.104, s32[]{:T(128)} %get-tuple-element.112, s32[512]{0:T(512)S(1)} %add_multiply_fusion.2), kind=kLoop, calls=%fused_computation.25.clone.1 | loop fusion | flops 9175040 | bytes 527360 | tf_op jit(solution)/shard_map/while/body/jit(dynamic_update_index_in_dim)/dynamic_update_slice | solution.py:46
  24.1 0.6 dynamic_slice.8
  24.7 0.6 add_multiply_fusion.2
  25.4 5.9 %fusion.37 = bf16[7,512,512]{2,1,0:T(8,128)(2,1)} fusion(bf16[7,512,512]{2,1,0:T(8,128)(2,1)} %get-tuple-element.105, s32[]{:T(128)} %get-tuple-element.104, s32[]{:T(128)} %get-tuple-element.112, s32[512]{0:T(512)S(1)} %add_multiply_fusion.2), kind=kLoop, calls=%fused_computation.25.clone.1 | loop fusion | flops 9175040 | bytes 527360 | tf_op jit(solution)/shard_map/while/body/jit(dynamic_update_index_in_dim)/dynamic_update_slice | solution.py:46
  31.2 0.6 dynamic_slice.8
  31.8 0.6 add_multiply_fusion.2
  32.5 5.9 %fusion.37 = bf16[7,512,512]{2,1,0:T(8,128)(2,1)} fusion(bf16[7,512,512]{2,1,0:T(8,128)(2,1)} %get-tuple-element.105, s32[]{:T(128)} %get-tuple-element.104, s32[]{:T(128)} %get-tuple-element.112, s32[512]{0:T(512)S(1)} %add_multiply_fusion.2), kind=kLoop, calls=%fused_computation.25.clone.1 | loop fusion | flops 9175040 | bytes 527360 | tf_op jit(solution)/shard_map/while/body/jit(dynamic_update_index_in_dim)/dynamic_update_slice | solution.py:46
  38.3 0.6 dynamic_slice.8
  38.9 0.6 add_multiply_fusion.2
  39.6 5.8 %fusion.37 = bf16[7,512,512]{2,1,0:T(8,128)(2,1)} fusion(bf16[7,512,512]{2,1,0:T(8,128)(2,1)} %get-tuple-element.105, s32[]{:T(128)} %get-tuple-element.104, s32[]{:T(128)} %get-tuple-element.112, s32[512]{0:T(512)S(1)} %add_multiply_fusion.2), kind=kLoop, calls=%fused_computation.25.clone.1 | loop fusion | flops 9175040 | bytes 527360 | tf_op jit(solution)/shard_map/while/body/jit(dynamic_update_index_in_dim)/dynamic_update_slice | solution.py:46
  45.4 0.6 dynamic_slice.8
  46.0 0.6 add_multiply_fusion.2
  46.6 5.9 %fusion.37 = bf16[7,512,512]{2,1,0:T(8,128)(2,1)} fusion(bf16[7,512,512]{2,1,0:T(8,128)(2,1)} %get-tuple-element.105, s32[]{:T(128)} %get-tuple-element.104, s32[]{:T(128)} %get-tuple-element.112, s32[512]{0:T(512)S(1)} %add_multiply_fusion.2), kind=kLoop, calls=%fused_computation.25.clone.1 | loop fusion | flops 9175040 | bytes 527360 | tf_op jit(solution)/shard_map/while/body/jit(dynamic_update_index_in_dim)/dynamic_update_slice | solution.py:46
  52.5 0.6 dynamic_slice.8
  53.1 0.6 add_multiply_fusion.2
  53.7 5.9 %fusion.37 = bf16[7,512,512]{2,1,0:T(8,128)(2,1)} fusion(bf16[7,512,512]{2,1,0:T(8,128)(2,1)} %get-tuple-element.105, s32[]{:T(128)} %get-tuple-element.104, s32[]{:T(128)} %get-tuple-element.112, s32[512]{0:T(512)S(1)} %add_multiply_fusion.2), kind=kLoop, calls=%fused_computation.25.clone.1 | loop fusion | flops 9175040 | bytes 527360 | tf_op jit(solution)/shard_map/while/body/jit(dynamic_update_index_in_dim)/dynamic_update_slice | solution.py:46
  59.6 0.0 copy-done
  59.6 0.0 copy-start.1
  59.6 0.0 copy-start.2
  59.6 3.2 %fusion.25 = f32[256,512]{0,1:T(8,128)S(1)} fusion(bf16[3584,512]{1,0:T(8,128)(2,1)} %bitcast.20, bf16[1,256,3584]{2,1,0:T(8,128)(2,1)S(1)} %copy-done), kind=kOutput, calls=%fused_computation.30 | convolution fusion | flops 939655168 | bytes 6029312 | tf_op jit(solution)/shard_map/dot_general | solution.py:48
  62.8 1.0 copy.8
  63.8 0.0 reduce-scatter.4.cloned.1.call-update
  64.6 76.2 %reduce-scatter.4.cloned.1.call-done = f32[16,512]{1,0:T(8,128)} async-done(((f32[256,512]{1,0:T(8,128)}), f32[16,512]{1,0:T(8,128)}) %reduce-scatter.4.cloned.1.call-update) | async-done | bytes 32784
  140.8 0.9 copy.9
  141.7 39.7 %psum.7 = bf16[16,512]{0,1:T(8,128)(2,1)S(1)} all-reduce(f32[16,512]{0,1:T(8,128)S(1)} %copy.9), channel_id=1, replica_groups=mesh['tensor'=8,'replica'=16,'fsdp'=8] {'tensor'}, use_global_device_ids=true, to_apply=%region_3.4 | all-reduce | flops 8192 | bytes 49152 | tf_op jit(solution)/shard_map/psum | solution.py:52
  181.3 0.0 copy-done.1
  181.3 0.0 copy-done.2
  181.4 4.0 %multiply_divide_fusion = (f32[16,3584]{1,0:T(8,128)}, f32[16,3584]{1,0:T(8,128)}, f32[16,3584]{1,0:T(8,128)}) fusion(f32[]{:T(128)} %bitcast.6, f32[]{:T(128)} %bitcast.5, f32[16,3584]{1,0:T(8,128)S(1)} %copy-done.1, f32[16,3584]{1,0:T(8,128)S(1)} %copy-done.2, bf16[16,512]{0,1:T(8,128)(2,1)S(1)} %psum.7, bf16[3584,512]{1,0:T(8,128)(2,1)} %bitcast.21), kind=kOutput, calls=%fused_computation.33 | convolution fusion | flops 59351040 | bytes 4833288 | tf_op jit(solution)/shard_map/dot_general | solution.py:54
  (2 shorter events, 0.0 us)
Async XLA Ops:
  7.2 52.4 %copy-start = (bf16[1,256,3584]{2,1,0:T(8,128)(2,1)S(1)}, bf16[1,256,3584]{2,1,0:T(8,128)(2,1)}, u32[]{:S(2)}) copy-start(bf16[1,256,3584]{2,1,0:T(8,128)(2,1)} %param.7) | copy-start | bytes 5505028
  7.2 133.6 %reduce-scatter.4.cloned.1.call-start = ((), (), s32[]{:S(2)}) async-start(), calls=%async_computation.1 | async-start | bytes 557056
  59.6 121.7 %copy-start.1 = (f32[16,3584]{1,0:T(8,128)S(1)}, f32[16,3584]{1,0:T(8,128)}, u32[]{:S(2)}) copy-start(f32[16,3584]{1,0:T(8,128)} %param.11) | copy-start | bytes 688132
  59.6 121.8 %copy-start.2 = (f32[16,3584]{1,0:T(8,128)S(1)}, f32[16,3584]{1,0:T(8,128)}, u32[]{:S(2)}) copy-start(f32[16,3584]{1,0:T(8,128)} %param.10) | copy-start | bytes 688132
Sparse Core Ops, SparseCore 0:
  64.0 76.7 reduce-scatter.3
where the time goes:
time: 194 us; the launch traced here: 192 us
  waiting for transfers between devices  76.2 us (39%)
  other arithmetic  45.5 us (23%)
  blocking collectives  39.7 us (20%)
  between operations  16.1 us (8%)
  local copies, waits for them, and re-layouts  7.34 us (4%)
  matrix products  7.21 us (4%)
    unnamed x2, waiting for transfers between devices  76.2 us
    dynamic_update_slice x7, other arithmetic, per_device(): lax.map(lambda first: projection_block(first, piece_cols, RANK, seeds), s...  41 us
    psum x1, blocking collectives, per_device(): sketch = lax.psum(share, 'tensor')  39.7 us
    mul x7, other arithmetic, projection_block(): counter = (column * jnp.int32(rank) + entry) * jnp.int32(2)  4.54 us
    dynamic_slice x7, local copies, waits for them, and re-layouts, per_device(): lax.map(lambda first: projection_block(first, piece_cols, RANK, seeds), s...  4.08 us
    dot_general x1, matrix products, per_device(): lax.dot_general(sketch_rounded, projection, (((1,), (1,)), ((), ())), pre...  3.96 us
  transfers between devices with their start and end apart: 1, of which 1 were waited for; matrix products, arithmetic and copies ran while one was open for 0% of the time, Pallas kernels for 0%

commit v1 on v0

v1 whole, which is shorter than its diff:
```python
import jax
import jax.numpy as jnp
from jax import lax
from jax.experimental import pallas as pl
from jax.experimental.pallas import tpu as pltpu
from jax.sharding import PartitionSpec as P

RANK = 512
COLUMNS = 3584
WIDTH = 128
DEPTH = 512
CHUNKS = RANK // WIDTH
BLOCKS = COLUMNS // DEPTH
STEPS = CHUNKS * BLOCKS
WEYL = -1640531535
MESH = pl.DeviceIdType.MESH
SINE = (6.28317941 / 16, -41.33894249 / 16, 81.39535834 / 16, -71.47469135 / 16)


def srl(value, bits):
    return lax.shift_right_logical(value, jnp.full_like(value, bits))


def scramble(value):
    value = value ^ srl(value, 16)
    value = value * jnp.int32(-2048144789)
    value = value ^ srl(value, 13)
    value = value * jnp.int32(-1028477387)
    return value ^ srl(value, 16)


def entries(counted, seed_key):
    hash_a = scramble(counted ^ seed_key)
    hash_b = scramble((counted + jnp.int32(WEYL)) ^ seed_key)
    negative_log = 16.635532333438686 - jnp.log(srl(hash_a, 8).astype(jnp.float32) + 0.5)
    radius = negative_log * lax.rsqrt(jnp.maximum(negative_log, 1e-30))
    turn = lax.shift_right_arithmetic(hash_b, jnp.full_like(hash_b, 8)).astype(jnp.float32) + 0.5
    z = 0.25 - jnp.abs(turn) * (1.0 / 16777216.0)
    square = z * z
    poly = SINE[3] * square + SINE[2]
    poly = poly * square + SINE[1]
    poly = poly * square + SINE[0]
    return (poly * z) * radius


def kernel(
    gradient_ref, seeds_ref, out_ref,
    grad, proj, base, acc, got1, out2, got2, out3, got3, sketch,
    grad_sem, send1, recv1, send2, recv2, send3, recv3,
):
    tensor = lax.axis_index("tensor")
    replica = lax.axis_index("replica")
    core = lax.rem(tensor, 2)
    z_hi = lax.div(tensor, 2)
    x = lax.div(replica, 2)
    z_lo = lax.rem(replica, 2)
    same = core == z_lo
    z = z_hi * 2 + z_lo

    def x_peer(step):
        return lax.rem(x + step, 8)

    barrier = pltpu.get_barrier_semaphore()
    pl.semaphore_signal(
        barrier, inc=1, device_id={"tensor": z_hi * 2 + 1 - core}, device_id_type=MESH
    )
    for step in range(1, 8):
        pl.semaphore_signal(
            barrier, inc=1, device_id={"replica": x_peer(step) * 2 + z_lo}, device_id_type=MESH
        )
    for far in range(8):
        far_hi, far_lo = far // 2, far % 2

        @pl.when(jnp.logical_or(far != z, jnp.logical_not(same)))
        def _():
            pl.semaphore_signal(
                barrier,
                inc=1,
                device_id={"tensor": far_hi * 2 + z_lo, "replica": x * 2 + far_lo},
                device_id_type=MESH,
            )

    def grad_copy(block):
        return pltpu.make_async_copy(
            gradient_ref.at[:, pl.ds(block * DEPTH, DEPTH)], grad.at[block], grad_sem.at[block]
        )

    for block in range(BLOCKS):
        grad_copy(block).start()

    seed_key = seeds_ref[0] ^ (seeds_ref[1] * jnp.int32(668265263))
    rows = lax.broadcasted_iota(jnp.int32, (DEPTH, WIDTH), 0)
    lanes = lax.broadcasted_iota(jnp.int32, (DEPTH, WIDTH), 1)
    base[...] = (rows * jnp.int32(RANK) + lanes) * jnp.int32(2) * jnp.int32(WEYL)
    first_column = tensor * COLUMNS

    def generate(index):
        chunk = lax.div(index, BLOCKS)
        block = lax.rem(index, BLOCKS)
        column = first_column + block * DEPTH
        offset = (column * jnp.int32(RANK) + chunk * WIDTH) * jnp.int32(2) * jnp.int32(WEYL)
        proj[index] = entries(base[...] + offset, seed_key).astype(jnp.bfloat16)

    def multiply(index):
        chunk = lax.div(index, BLOCKS)
        block = lax.rem(index, BLOCKS)
        part = jnp.dot(grad[block], proj[index], preferred_element_type=jnp.float32)
        part = part.reshape(8, 2, 16, WIDTH)
        acc[chunk] = jnp.where(block == 0, 0.0, acc[chunk]) + part

    def copy1(chunk):
        return pltpu.make_async_remote_copy(
            src_ref=acc.at[chunk, :, 1 - core],
            dst_ref=got1.at[chunk],
            send_sem=send1.at[chunk],
            recv_sem=recv1.at[chunk],
            device_id={"tensor": z_hi * 2 + 1 - core},
            device_id_type=MESH,
        )

    def copy2(chunk, step):
        return pltpu.make_async_remote_copy(
            src_ref=out2.at[chunk, x_peer(step)],
            dst_ref=got2.at[chunk, x],
            send_sem=send2.at[chunk, step],
            recv_sem=recv2.at[chunk, x],
            device_id={"replica": x_peer(step) * 2 + z_lo},
            device_id_type=MESH,
        )

    def arrive2(chunk, step):
        return pltpu.make_async_remote_copy(
            src_ref=out2.at[chunk, x],
            dst_ref=got2.at[chunk, x_peer(step)],
            send_sem=send2.at[chunk, step],
            recv_sem=recv2.at[chunk, x_peer(step)],
            device_id={"replica": x_peer(step) * 2 + z_lo},
            device_id_type=MESH,
        )

    def copy3(chunk, target):
        return pltpu.make_async_remote_copy(
            src_ref=out3.at[chunk],
            dst_ref=got3.at[chunk, z],
            send_sem=send3.at[chunk, target],
            recv_sem=recv3.at[chunk, z],
            device_id={"tensor": target, "replica": x * 2 + core},
            device_id_type=MESH,
        )

    def arrive3(chunk, far):
        return pltpu.make_async_remote_copy(
            src_ref=out3.at[chunk],
            dst_ref=got3.at[chunk, far],
            send_sem=send3.at[chunk, far],
            recv_sem=recv3.at[chunk, far],
            device_id={"tensor": (far // 2) * 2 + z_lo, "replica": x * 2 + far % 2},
            device_id_type=MESH,
        )

    def not_self(target):
        return jnp.logical_or(target != tensor, jnp.logical_not(same))

    def stage1(chunk):
        copy1(chunk).start()

    def stage2(chunk):
        copy1(chunk).wait_recv()
        total = acc[chunk, :, core] + got1[chunk]
        out2[chunk] = total.astype(jnp.bfloat16)
        for step in range(1, 8):
            copy2(chunk, step).start()

    def stage3(chunk):
        total = acc[chunk, x, core] + got1[chunk, x]
        for step in range(1, 8):
            arrive2(chunk, step).wait_recv()
            total = total + got2[chunk, x_peer(step)].astype(jnp.float32)
        out3[chunk] = total.astype(jnp.bfloat16)
        for target in range(8):

            @pl.when(not_self(target))
            def _():
                copy3(chunk, target).start()

        @pl.when(same)
        def _():
            got3[chunk, z] = out3[chunk]

    def finish(chunk):
        for far in range(8):

            @pl.when(jnp.logical_or(far != z, jnp.logical_not(same)))
            def _():
                arrive3(chunk, far).wait_recv()

        total = jnp.zeros((16, WIDTH), jnp.float32)
        for far in range(8):
            total = total + got3[chunk, far].astype(jnp.float32)
        sketch[chunk] = (total * (1.0 / 16)).astype(jnp.bfloat16)

    def back(chunk, index):
        return lax.dot_general(
            sketch[chunk],
            proj[chunk * BLOCKS + index],
            (((1,), (1,)), ((), ())),
            preferred_element_type=jnp.float32,
        )

    generate(0)
    for block in range(BLOCKS):
        grad_copy(block).wait()

    pl.semaphore_wait(barrier, jnp.where(same, 15, 16))

    def body(index, carry):
        multiply(index - 1)
        generate(index)
        chunk = lax.div(index, BLOCKS) - 1
        phase = lax.rem(index, BLOCKS)
        for at, work in ((0, stage1), (2, stage2), (4, stage3), (6, finish)):

            @pl.when(jnp.logical_and(chunk >= 0, phase == at))
            def _():
                work(chunk)

        return carry

    lax.fori_loop(1, STEPS, body, 0)
    last = CHUNKS - 1
    multiply(STEPS - 1)
    stage1(last)
    stage2(last)
    for block in range(BLOCKS):
        total = back(0, block)
        for chunk in range(1, last):
            total = total + back(chunk, block)
        out_ref[:, block * DEPTH : (block + 1) * DEPTH] = total
    stage3(last)
    finish(last)
    for block in range(BLOCKS):
        out_ref[:, block * DEPTH : (block + 1) * DEPTH] += back(last, block)
    for chunk in range(CHUNKS):
        copy1(chunk).wait_send()
        for step in range(1, 8):
            copy2(chunk, step).wait_send()
        for target in range(8):

            @pl.when(not_self(target))
            def _():
                copy3(chunk, target).wait_send()


def per_device(gradients, seeds, adam_step, first_moment, second_moment):
    gradient = gradients[0]
    dma = pltpu.SemaphoreType.DMA
    estimate = pl.pallas_call(
        kernel,
        out_shape=jax.ShapeDtypeStruct((16, COLUMNS), jnp.float32),
        in_specs=[
            pl.BlockSpec(memory_space=pl.ANY),
            pl.BlockSpec(memory_space=pltpu.SMEM),
        ],
        out_specs=pl.BlockSpec(memory_space=pltpu.VMEM),
        scratch_shapes=[
            pltpu.VMEM((BLOCKS, 256, DEPTH), jnp.bfloat16),
            pltpu.VMEM((STEPS, DEPTH, WIDTH), jnp.bfloat16),
            pltpu.VMEM((DEPTH, WIDTH), jnp.int32),
            pltpu.VMEM((CHUNKS, 8, 2, 16, WIDTH), jnp.float32),
            pltpu.VMEM((CHUNKS, 8, 16, WIDTH), jnp.float32),
            pltpu.VMEM((CHUNKS, 8, 16, WIDTH), jnp.bfloat16),
            pltpu.VMEM((CHUNKS, 8, 16, WIDTH), jnp.bfloat16),
            pltpu.VMEM((CHUNKS, 16, WIDTH), jnp.bfloat16),
            pltpu.VMEM((CHUNKS, 8, 16, WIDTH), jnp.bfloat16),
            pltpu.VMEM((CHUNKS, 16, WIDTH), jnp.bfloat16),
            dma((BLOCKS,)),
            dma((CHUNKS,)),
            dma((CHUNKS,)),
            dma((CHUNKS, 8)),
            dma((CHUNKS, 8)),
            dma((CHUNKS, 8)),
            dma((CHUNKS, 8)),
        ],
        compiler_params=pltpu.CompilerParams(
            collective_id=0, has_side_effects=True, vmem_limit_bytes=24 << 20
        ),
        cost_estimate=pl.CostEstimate(
            flops=2 * 256 * COLUMNS * RANK, bytes_accessed=3 << 20, transcendentals=0
        ),
    )(gradient, seeds)
    new_first = 0.9 * first_moment + 0.1 * estimate
    new_second = 0.95 * second_moment + 0.05 * estimate * estimate
    step_float = adam_step[0].astype(jnp.float32)
    fix_first = 1.0 - jnp.power(jnp.float32(0.9), step_float)
    fix_second = 1.0 - jnp.power(jnp.float32(0.95), step_float)
    step_update = new_first / fix_first / (jnp.sqrt(new_second / fix_second) + 1e-08)
    return (new_first, new_second, step_update)


def solution(mesh):
    rows = P(("fsdp", "replica"), "tensor")
    return jax.shard_map(
        per_device,
        mesh=mesh,
        in_specs=(P("replica", "fsdp", "tensor"), P(), P(), rows, rows),
        out_specs=(rows, rows, rows),
        check_vma=False,
    )
```

time: 194 us -> 75.9 us (0.39)
  waiting for transfers between devices: 76.2 us -> 0 us
  Pallas kernels: 0 us -> 71.2 us
  other arithmetic: 45.5 us -> 0.91 us
  blocking collectives: 39.7 us -> 0 us
  between operations: 16.1 us -> 1.39 us
  matrix products: 7.21 us -> 0 us
  local copies, waits for them, and re-layouts: 7.34 us -> 2.15 us
    unnamed x2 -> x0, waiting for transfers between devices: 76.2 us -> none
    pallas_call x0 -> x1, Pallas kernels: none -> 71.2 us  [per_device(): pl.pallas_call(kernel, out_shape=jax.ShapeDtypeStruct((16, COLUMNS), jnp....]
    dynamic_update_slice x7 -> x0, other arithmetic: 41 us -> none  [per_device(): lax.map(lambda first: projection_block(first, piece_cols, RANK, seeds), s...]
    psum x1 -> x0, blocking collectives: 39.7 us -> none  [per_device(): sketch = lax.psum(share, 'tensor')]
    dot_general x2 -> x0, matrix products: 7.21 us -> none  [the longest x1 3.96 us: per_device(): lax.dot_general(sketch_rounded, projection, (((1,), (1,)), ((), ())), pre...]
    mul x7 -> x0, other arithmetic: 4.54 us -> none  [projection_block(): counter = (column * jnp.int32(rank) + entry) * jnp.int32(2)]
    dynamic_slice x7 -> x0, local copies, waits for them, and re-layouts: 4.08 us -> none  [per_device(): lax.map(lambda first: projection_block(first, piece_cols, RANK, seeds), s...]
  transfers between devices with their start and end apart: 1 -> 0, of which waited for: 1 -> 0; matrix products, arithmetic and copies ran while one was open for 0% -> 0% of each run, Pallas kernels for 0% -> 0%
where the time goes in v1:
time: 75.9 us; the launch traced here: 75.7 us
  Pallas kernels  71.2 us (94%)
  local copies, waits for them, and re-layouts  2.15 us (3%)
  between operations  1.39 us (2%)
  other arithmetic  0.91 us (1%)
    pallas_call x1, Pallas kernels, per_device(): pl.pallas_call(kernel, out_shape=jax.ShapeDtypeStruct((16, COLUMNS), jnp....  71.2 us
    unnamed x8, local copies, waits for them, and re-layouts  2.15 us

profile of v1, /device:TPU:1, one launch (start us, length us, event | category | flops | bytes accessed | tf_op | source)
XLA Modules:
  0.0 75.7 jit_solution(8255505797507513035)
XLA Ops:
  1.4 0.0 copy-start
  1.4 1.5 %copy-done = bf16[1,256,3584]{2,1,0:T(8,128)(2,1)S(1)} copy-done((bf16[1,256,3584]{2,1,0:T(8,128)(2,1)S(1)}, bf16[1,256,3584]{2,1,0:T(8,128)(2,1)}, u32[]{:S(2)}) %copy-start) | copy-done | bytes 1835032
  2.9 0.0 copy-start.1
  2.9 0.7 copy-done.1
  3.5 0.0 copy-start.2
  3.5 0.0 copy-start.3
  3.5 71.2 %shard_map.76 = f32[16,3584]{1,0:T(8,128)S(1)} custom-call(bf16[256,3584]{1,0:T(8,128)(2,1)S(1)} %bitcast.3, s32[2]{0:T(128)S(1)} %copy-done.1), custom_call_target="tpu_custom_call" | custom-call | flops 939524096 | bytes 3145728 | tf_op jit(solution)/shard_map/pallas_call | solution.py:257
  74.8 0.0 copy-done.2
  74.8 0.0 copy-done.3
  74.8 0.9 %multiply_divide_fusion = (f32[16,3584]{1,0:T(8,128)}, f32[16,3584]{1,0:T(8,128)}, f32[16,3584]{1,0:T(8,128)}) fusion(f32[]{:T(128)} %bitcast.2, f32[]{:T(128)} %bitcast.1, f32[16,3584]{1,0:T(8,128)S(1)} %shard_map.76, f32[16,3584]{1,0:T(8,128)S(1)} %copy-done.2, f32[16,3584]{1,0:T(8,128)S(1)} %copy-done.3), kind=kLoop, calls=%fused_computation.2 | loop fusion | flops 630784 | bytes 1376264 | tf_op jit(solution)/shard_map/div | solution.py:296
Async XLA Ops:
  1.4 1.5 %copy-start = (bf16[1,256,3584]{2,1,0:T(8,128)(2,1)S(1)}, bf16[1,256,3584]{2,1,0:T(8,128)(2,1)}, u32[]{:S(2)}) copy-start(bf16[1,256,3584]{2,1,0:T(8,128)(2,1)} %param.5) | copy-start | bytes 5505028
  2.9 0.7 copy-start.1
  3.5 71.2 %copy-start.2 = (f32[16,3584]{1,0:T(8,128)S(1)}, f32[16,3584]{1,0:T(8,128)}, u32[]{:S(2)}) copy-start(f32[16,3584]{1,0:T(8,128)} %param.9) | copy-start | bytes 688132
  3.5 71.2 %copy-start.3 = (f32[16,3584]{1,0:T(8,128)S(1)}, f32[16,3584]{1,0:T(8,128)}, u32[]{:S(2)}) copy-start(f32[16,3584]{1,0:T(8,128)} %param.8) | copy-start | bytes 688132

commit v2 on v1

--- a/solution.py
+++ b/solution.py
@@ -7,11 +7,12 @@
 
 RANK = 512
 COLUMNS = 3584
-WIDTH = 128
-DEPTH = 512
+WIDTH = 256
+DEPTH = 256
+PIECE = 896
+PIECES = COLUMNS // PIECE
 CHUNKS = RANK // WIDTH
 BLOCKS = COLUMNS // DEPTH
-STEPS = CHUNKS * BLOCKS
 WEYL = -1640531535
 MESH = pl.DeviceIdType.MESH
 SINE = (6.28317941 / 16, -41.33894249 / 16, 81.39535834 / 16, -71.47469135 / 16)
@@ -80,13 +81,13 @@
                 device_id_type=MESH,
             )
 
-    def grad_copy(block):
+    def grad_copy(piece):
         return pltpu.make_async_copy(
-            gradient_ref.at[:, pl.ds(block * DEPTH, DEPTH)], grad.at[block], grad_sem.at[block]
-        )
-
-    for block in range(BLOCKS):
-        grad_copy(block).start()
+            gradient_ref.at[:, pl.ds(piece * PIECE, PIECE)], grad.at[piece], grad_sem.at[piece]
+        )
+
+    for piece in range(PIECES):
+        grad_copy(piece).start()
 
     seed_key = seeds_ref[0] ^ (seeds_ref[1] * jnp.int32(668265263))
     rows = lax.broadcasted_iota(jnp.int32, (DEPTH, WIDTH), 0)
@@ -94,19 +95,27 @@
     base[...] = (rows * jnp.int32(RANK) + lanes) * jnp.int32(2) * jnp.int32(WEYL)
     first_column = tensor * COLUMNS
 
-    def generate(index):
-        chunk = lax.div(index, BLOCKS)
-        block = lax.rem(index, BLOCKS)
-        column = first_column + block * DEPTH
-        offset = (column * jnp.int32(RANK) + chunk * WIDTH) * jnp.int32(2) * jnp.int32(WEYL)
-        proj[index] = entries(base[...] + offset, seed_key).astype(jnp.bfloat16)
-
-    def multiply(index):
-        chunk = lax.div(index, BLOCKS)
-        block = lax.rem(index, BLOCKS)
-        part = jnp.dot(grad[block], proj[index], preferred_element_type=jnp.float32)
-        part = part.reshape(8, 2, 16, WIDTH)
-        acc[chunk] = jnp.where(block == 0, 0.0, acc[chunk]) + part
+    def generate(chunk, lower, upper):
+        def step(block, carry):
+            start = pl.multiple_of(block * DEPTH, DEPTH)
+            column = first_column + start
+            offset = (column * jnp.int32(RANK) + chunk * WIDTH) * jnp.int32(2) * jnp.int32(WEYL)
+            made = entries(base[...] + offset, seed_key).astype(jnp.bfloat16)
+            proj[chunk, pl.ds(start, DEPTH), :] = made
+            return carry
+
+        lax.fori_loop(lower, upper, step, 0)
+
+    def multiply(chunk):
+        part = None
+        for piece in range(PIECES):
+            term = jnp.dot(
+                grad[piece],
+                proj[chunk, piece * PIECE : (piece + 1) * PIECE, :],
+                preferred_element_type=jnp.float32,
+            )
+            part = term if part is None else part + term
+        acc[chunk] = part.reshape(8, 2, 16, WIDTH)
 
     def copy1(chunk):
         return pltpu.make_async_remote_copy(
@@ -167,16 +176,16 @@
     def stage2(chunk):
         copy1(chunk).wait_recv()
         total = acc[chunk, :, core] + got1[chunk]
-        out2[chunk] = total.astype(jnp.bfloat16)
+        out2[chunk] = total
         for step in range(1, 8):
             copy2(chunk, step).start()
 
     def stage3(chunk):
-        total = acc[chunk, x, core] + got1[chunk, x]
+        total = out2[chunk, x]
         for step in range(1, 8):
             arrive2(chunk, step).wait_recv()
-            total = total + got2[chunk, x_peer(step)].astype(jnp.float32)
-        out3[chunk] = total.astype(jnp.bfloat16)
+            total = total + got2[chunk, x_peer(step)]
+        out3[chunk] = total
         for target in range(8):
 
             @pl.when(not_self(target))
@@ -196,50 +205,38 @@
 
         total = jnp.zeros((16, WIDTH), jnp.float32)
         for far in range(8):
-            total = total + got3[chunk, far].astype(jnp.float32)
+            total = total + got3[chunk, far]
         sketch[chunk] = (total * (1.0 / 16)).astype(jnp.bfloat16)
 
-    def back(chunk, index):
-        return lax.dot_general(
-            sketch[chunk],
-            proj[chunk * BLOCKS + index],
-            (((1,), (1,)), ((), ())),
-            preferred_element_type=jnp.float32,
-        )
-
-    generate(0)
-    for block in range(BLOCKS):
-        grad_copy(block).wait()
-
+    def back(chunk, first):
+        for piece in range(PIECES):
+            part = slice(piece * PIECE, (piece + 1) * PIECE)
+            term = lax.dot_general(
+                sketch[chunk],
+                proj[chunk, part, :],
+                (((1,), (1,)), ((), ())),
+                preferred_element_type=jnp.float32,
+            )
+            out_ref[:, part] = term if first else out_ref[:, part] + term
+
+    generate(0, 0, BLOCKS)
+    for piece in range(PIECES):
+        grad_copy(piece).wait()
+    multiply(0)
     pl.semaphore_wait(barrier, jnp.where(same, 15, 16))
-
-    def body(index, carry):
-        multiply(index - 1)
-        generate(index)
-        chunk = lax.div(index, BLOCKS) - 1
-        phase = lax.rem(index, BLOCKS)
-        for at, work in ((0, stage1), (2, stage2), (4, stage3), (6, finish)):
-
-            @pl.when(jnp.logical_and(chunk >= 0, phase == at))
-            def _():
-                work(chunk)
-
-        return carry
-
-    lax.fori_loop(1, STEPS, body, 0)
-    last = CHUNKS - 1
-    multiply(STEPS - 1)
-    stage1(last)
-    stage2(last)
-    for block in range(BLOCKS):
-        total = back(0, block)
-        for chunk in range(1, last):
-            total = total + back(chunk, block)
-        out_ref[:, block * DEPTH : (block + 1) * DEPTH] = total
-    stage3(last)
-    finish(last)
-    for block in range(BLOCKS):
-        out_ref[:, block * DEPTH : (block + 1) * DEPTH] += back(last, block)
+    stage1(0)
+    generate(1, 0, 4)
+    stage2(0)
+    generate(1, 4, BLOCKS)
+    multiply(1)
+    stage1(1)
+    stage3(0)
+    stage2(1)
+    finish(0)
+    stage3(1)
+    back(0, True)
+    finish(1)
+    back(1, False)
     for chunk in range(CHUNKS):
         copy1(chunk).wait_send()
         for step in range(1, 8):
@@ -252,28 +249,29 @@
 
 
 def per_device(gradients, seeds, adam_step, first_moment, second_moment):
-    gradient = gradients[0]
+    gradient = pltpu.with_memory_space_constraint(gradients[0], pltpu.HBM)
+    seeds = pltpu.with_memory_space_constraint(seeds, pltpu.HBM)
     dma = pltpu.SemaphoreType.DMA
     estimate = pl.pallas_call(
         kernel,
-        out_shape=jax.ShapeDtypeStruct((16, COLUMNS), jnp.float32),
+        out_shape=pltpu.VMEM((16, COLUMNS), jnp.float32),
         in_specs=[
-            pl.BlockSpec(memory_space=pl.ANY),
+            pl.BlockSpec(memory_space=pltpu.HBM),
             pl.BlockSpec(memory_space=pltpu.SMEM),
         ],
         out_specs=pl.BlockSpec(memory_space=pltpu.VMEM),
         scratch_shapes=[
-            pltpu.VMEM((BLOCKS, 256, DEPTH), jnp.bfloat16),
-            pltpu.VMEM((STEPS, DEPTH, WIDTH), jnp.bfloat16),
+            pltpu.VMEM((PIECES, 256, PIECE), jnp.bfloat16),
+            pltpu.VMEM((CHUNKS, COLUMNS, WIDTH), jnp.bfloat16),
             pltpu.VMEM((DEPTH, WIDTH), jnp.int32),
             pltpu.VMEM((CHUNKS, 8, 2, 16, WIDTH), jnp.float32),
             pltpu.VMEM((CHUNKS, 8, 16, WIDTH), jnp.float32),
-            pltpu.VMEM((CHUNKS, 8, 16, WIDTH), jnp.bfloat16),
-            pltpu.VMEM((CHUNKS, 8, 16, WIDTH), jnp.bfloat16),
+            pltpu.VMEM((CHUNKS, 8, 16, WIDTH), jnp.float32),
+            pltpu.VMEM((CHUNKS, 8, 16, WIDTH), jnp.float32),
+            pltpu.VMEM((CHUNKS, 16, WIDTH), jnp.float32),
+            pltpu.VMEM((CHUNKS, 8, 16, WIDTH), jnp.float32),
             pltpu.VMEM((CHUNKS, 16, WIDTH), jnp.bfloat16),
-            pltpu.VMEM((CHUNKS, 8, 16, WIDTH), jnp.bfloat16),
-            pltpu.VMEM((CHUNKS, 16, WIDTH), jnp.bfloat16),
-            dma((BLOCKS,)),
+            dma((PIECES,)),
             dma((CHUNKS,)),
             dma((CHUNKS,)),
             dma((CHUNKS, 8)),

time: 75.9 us -> 48.2 us (0.64)
  Pallas kernels: 71.2 us -> 45.7 us
  local copies, waits for them, and re-layouts: 2.15 us -> 0.01 us
    pallas_call x1, Pallas kernels: 71.2 us -> 45.7 us  [per_device(): pl.pallas_call(kernel, out_shape=pltpu.VMEM((16, COLUMNS), jnp.float32),...]
    unnamed x8 -> x4, local copies, waits for them, and re-layouts: 2.15 us -> 0.01 us
where the time goes in v2:
time: 48.2 us; the launch traced here: 48.1 us
  Pallas kernels  45.7 us (95%)
  between operations  1.45 us (3%)
  other arithmetic  0.91 us (2%)
    pallas_call x1, Pallas kernels, per_device(): pl.pallas_call(kernel, out_shape=pltpu.VMEM((16, COLUMNS), jnp.float32),...  45.7 us

profile of v2, /device:TPU:1, one launch (start us, length us, event | category | flops | bytes accessed | tf_op | source)
XLA Modules:
  0.0 48.1 jit_solution(9387816529252748470)
XLA Ops:
  0.6 0.0 copy-start
  0.6 0.0 copy-start.1
  1.4 45.7 %shard_map.76 = f32[16,3584]{1,0:T(8,128)S(1)} custom-call(bf16[256,3584]{1,0:T(8,128)(2,1)} %bitcast.3, s32[2]{0:T(128)} %seeds_ref.1), custom_call_target="tpu_custom_call" | custom-call | flops 939524096 | bytes 3145728 | tf_op jit(solution)/shard_map/pallas_call | solution.py:255
  47.1 0.0 copy-done
  47.1 0.0 copy-done.1
  47.1 0.9 %multiply_divide_fusion = (f32[16,3584]{1,0:T(8,128)}, f32[16,3584]{1,0:T(8,128)}, f32[16,3584]{1,0:T(8,128)}) fusion(f32[]{:T(128)} %bitcast.2, f32[]{:T(128)} %bitcast.1, f32[16,3584]{1,0:T(8,128)S(1)} %shard_map.76, f32[16,3584]{1,0:T(8,128)S(1)} %copy-done, f32[16,3584]{1,0:T(8,128)S(1)} %copy-done.1), kind=kLoop, calls=%fused_computation.2 | loop fusion | flops 630784 | bytes 1376264 | tf_op jit(solution)/shard_map/div | solution.py:294
Async XLA Ops:
  0.6 46.5 %copy-start = (f32[16,3584]{1,0:T(8,128)S(1)}, f32[16,3584]{1,0:T(8,128)}, u32[]{:S(2)}) copy-start(f32[16,3584]{1,0:T(8,128)} %param.9) | copy-start | bytes 688132
  0.6 46.5 %copy-start.1 = (f32[16,3584]{1,0:T(8,128)S(1)}, f32[16,3584]{1,0:T(8,128)}, u32[]{:S(2)}) copy-start(f32[16,3584]{1,0:T(8,128)} %param.8) | copy-start | bytes 688132

commit v3 on v2

v3 whole, which is shorter than its diff:
```python
import math

import jax
import jax.numpy as jnp
from jax import lax
from jax.experimental import pallas as pl
from jax.experimental.pallas import tpu as pltpu
from jax.sharding import PartitionSpec as P

RANK = 512
COLUMNS = 3584
WIDTHS = (384, 128)
STARTS = (0, 384)
CHUNKS = len(WIDTHS)
DEPTH = 512
BLOCKS = COLUMNS // DEPTH
PIECE = 896
PIECES = COLUMNS // PIECE
X_ORDER = (4, 3, 5, 2, 6, 1, 7)
Z_ORDER = ((2, 0), (2, 1), (1, 0), (1, 1), (3, 0), (3, 1), (0, 1), (0, 0))
WEYL = -1640531535
MESH = pl.DeviceIdType.MESH
SINE = (6.28317941 / 16, -41.33894249 / 16, 81.39535834 / 16, -71.47469135 / 16)


def srl(value, bits):
    return lax.shift_right_logical(value, jnp.full_like(value, bits))


def scramble(value):
    value = value ^ srl(value, 16)
    value = value * jnp.int32(-2048144789)
    value = value ^ srl(value, 13)
    value = value * jnp.int32(-1028477387)
    return value ^ srl(value, 16)


def entries(counted, seed_key):
    hash_a = scramble(counted ^ seed_key)
    hash_b = scramble((counted + jnp.int32(WEYL)) ^ seed_key)
    negative_log = 16.635532333438686 - jnp.log(srl(hash_a, 8).astype(jnp.float32) + 0.5)
    radius = negative_log * lax.rsqrt(jnp.maximum(negative_log, 1e-30))
    turn = lax.shift_right_arithmetic(hash_b, jnp.full_like(hash_b, 8)).astype(jnp.float32) + 0.5
    z = 0.25 - jnp.abs(turn) * (1.0 / 16777216.0)
    square = z * z
    poly = SINE[3] * square + SINE[2]
    poly = poly * square + SINE[1]
    poly = poly * square + SINE[0]
    return (poly * z) * radius


def kernel(gradient_ref, seeds_ref, step_ref, out_ref, fix_ref, *scratch):
    grad, base, seeds, when = scratch[:4]
    per_chunk = [scratch[4 + i * CHUNKS : 4 + (i + 1) * CHUNKS] for i in range(7)]
    proj, acc, got1, out2, got2, out3, got3 = per_chunk
    sketch = scratch[4 + 7 * CHUNKS : 4 + 8 * CHUNKS]
    grad_sem, small_sem, send1, recv1, send2, recv2, send3, recv3 = scratch[4 + 8 * CHUNKS :]
    tensor = lax.axis_index("tensor")
    replica = lax.axis_index("replica")
    core = lax.rem(tensor, 2)
    z_hi = lax.div(tensor, 2)
    x = lax.div(replica, 2)
    z_lo = lax.rem(replica, 2)
    same = core == z_lo
    z = z_hi * 2 + z_lo

    def x_peer(step):
        return lax.rem(x + step, 8)

    seeds_copy = pltpu.make_async_copy(seeds_ref, seeds, small_sem.at[0])
    seeds_copy.start()

    barrier = pltpu.get_barrier_semaphore()
    pl.semaphore_signal(
        barrier, inc=1, device_id={"tensor": z_hi * 2 + 1 - core}, device_id_type=MESH
    )
    for step in range(1, 8):
        pl.semaphore_signal(
            barrier, inc=1, device_id={"replica": x_peer(step) * 2 + z_lo}, device_id_type=MESH
        )
    for far in range(8):
        far_hi, far_lo = far // 2, far % 2

        @pl.when(jnp.logical_or(far != z, jnp.logical_not(same)))
        def _():
            pl.semaphore_signal(
                barrier,
                inc=1,
                device_id={"tensor": far_hi * 2 + z_lo, "replica": x * 2 + far_lo},
                device_id_type=MESH,
            )

    def grad_copy(piece):
        return pltpu.make_async_copy(
            gradient_ref.at[:, pl.ds(piece * PIECE, PIECE)], grad.at[piece], grad_sem.at[piece]
        )

    for piece in range(PIECES):
        grad_copy(piece).start()

    rows = lax.broadcasted_iota(jnp.int32, base.shape, 0)
    lanes = lax.broadcasted_iota(jnp.int32, base.shape, 1)
    base[...] = (rows * jnp.int32(RANK) + lanes) * jnp.int32(2) * jnp.int32(WEYL)
    seeds_copy.wait()
    seed_key = seeds[0] ^ (seeds[1] * jnp.int32(668265263))
    first_column = tensor * COLUMNS

    def generate(chunk, lower, upper):
        def step(block, carry):
            start = pl.multiple_of(block * DEPTH, DEPTH)
            column = first_column + start
            offset = (column * jnp.int32(RANK) + STARTS[chunk]) * jnp.int32(2) * jnp.int32(WEYL)
            made = entries(base[:, : WIDTHS[chunk]] + offset, seed_key).astype(jnp.bfloat16)
            proj[chunk][pl.ds(start, DEPTH), :] = made
            return carry

        lax.fori_loop(lower, upper, step, 0)

    def multiply(chunk):
        part = None
        for piece in range(PIECES):
            term = jnp.dot(
                grad[piece],
                proj[chunk][piece * PIECE : (piece + 1) * PIECE, :],
                preferred_element_type=jnp.float32,
            )
            part = term if part is None else part + term
        acc[chunk][...] = part.reshape(8, 2, 16, WIDTHS[chunk])

    def copy1(chunk):
        return pltpu.make_async_remote_copy(
            src_ref=acc[chunk].at[:, 1 - core],
            dst_ref=got1[chunk],
            send_sem=send1.at[chunk],
            recv_sem=recv1.at[chunk],
            device_id={"tensor": z_hi * 2 + 1 - core},
            device_id_type=MESH,
        )

    def copy2(chunk, step):
        return pltpu.make_async_remote_copy(
            src_ref=out2[chunk].at[x_peer(step)],
            dst_ref=got2[chunk].at[x],
            send_sem=send2.at[chunk, step],
            recv_sem=recv2.at[chunk, x],
            device_id={"replica": x_peer(step) * 2 + z_lo},
            device_id_type=MESH,
        )

    def arrive2(chunk, step):
        return pltpu.make_async_remote_copy(
            src_ref=out2[chunk].at[x],
            dst_ref=got2[chunk].at[x_peer(step)],
            send_sem=send2.at[chunk, step],
            recv_sem=recv2.at[chunk, x_peer(step)],
            device_id={"replica": x_peer(step) * 2 + z_lo},
            device_id_type=MESH,
        )

    def copy3(chunk, number):
        ahead, other = Z_ORDER[number]
        target_core = 1 - core if other else core
        return pltpu.make_async_remote_copy(
            src_ref=out3[chunk],
            dst_ref=got3[chunk].at[z],
            send_sem=send3.at[chunk, number],
            recv_sem=recv3.at[chunk, z],
            device_id={
                "tensor": lax.rem(z_hi + ahead, 4) * 2 + target_core,
                "replica": x * 2 + core,
            },
            device_id_type=MESH,
        )

    def arrive3(chunk, far):
        return pltpu.make_async_remote_copy(
            src_ref=out3[chunk],
            dst_ref=got3[chunk].at[far],
            send_sem=send3.at[chunk, far],
            recv_sem=recv3.at[chunk, far],
            device_id={"tensor": (far // 2) * 2 + z_lo, "replica": x * 2 + far % 2},
            device_id_type=MESH,
        )

    def stage1(chunk):
        copy1(chunk).start()

    def stage2(chunk):
        copy1(chunk).wait_recv()
        out2[chunk][...] = acc[chunk][:, core] + got1[chunk][...]
        for step in X_ORDER:
            copy2(chunk, step).start()

    def stage3(chunk):
        total = out2[chunk][x]
        for step in range(1, 8):
            arrive2(chunk, step).wait_recv()
            total = total + got2[chunk][x_peer(step)]
        out3[chunk][...] = total
        for number in range(7):
            copy3(chunk, number).start()

        @pl.when(jnp.logical_not(same))
        def _():
            copy3(chunk, 7).start()

        @pl.when(same)
        def _():
            got3[chunk][z] = out3[chunk][...]

    def finish(chunk):
        for far in range(8):

            @pl.when(jnp.logical_or(far != z, jnp.logical_not(same)))
            def _():
                arrive3(chunk, far).wait_recv()

        total = got3[chunk][0]
        for far in range(1, 8):
            total = total + got3[chunk][far]
        sketch[chunk][...] = (total * (1.0 / 16)).astype(jnp.bfloat16)

    def back(chunk, first):
        for piece in range(PIECES):
            part = slice(piece * PIECE, (piece + 1) * PIECE)
            term = lax.dot_general(
                sketch[chunk][...],
                proj[chunk][part, :],
                (((1,), (1,)), ((), ())),
                preferred_element_type=jnp.float32,
            )
            out_ref[:, part] = term if first else out_ref[:, part] + term

    generate(0, 0, BLOCKS)
    for piece in range(PIECES):
        grad_copy(piece).wait()
    multiply(0)
    pl.semaphore_wait(barrier, jnp.where(same, 15, 16))
    stage1(0)
    generate(1, 0, 4)
    stage2(0)
    generate(1, 4, BLOCKS)
    multiply(1)
    stage1(1)
    stage2(1)
    stage3(0)
    steps = jnp.broadcast_to(step_ref[...], (8, 128)).astype(jnp.float32)
    first = lax.broadcasted_iota(jnp.int32, (8, 128), 0) < 4
    power = jnp.exp(steps * jnp.where(first, math.log(0.9), math.log(0.95)))
    fix_ref[...] = jnp.tile(1.0 / (1.0 - power), (1, COLUMNS // 128))
    stage3(1)
    finish(0)
    back(0, True)
    finish(1)
    back(1, False)
    for chunk in range(CHUNKS):
        copy1(chunk).wait_send()
        for step in X_ORDER:
            copy2(chunk, step).wait_send()
        for number in range(7):
            copy3(chunk, number).wait_send()

        @pl.when(jnp.logical_not(same))
        def _():
            copy3(chunk, 7).wait_send()


def per_device(gradients, seeds, adam_step, first_moment, second_moment):
    gradient = pltpu.with_memory_space_constraint(gradients[0], pltpu.HBM)
    seeds = pltpu.with_memory_space_constraint(seeds, pltpu.HBM)
    dma = pltpu.SemaphoreType.DMA
    estimate, fix = pl.pallas_call(
        kernel,
        out_shape=(pltpu.VMEM((16, COLUMNS), jnp.float32), pltpu.VMEM((8, COLUMNS), jnp.float32)),
        in_specs=[
            pl.BlockSpec(memory_space=pltpu.HBM),
            pl.BlockSpec(memory_space=pltpu.HBM),
            pl.BlockSpec(memory_space=pltpu.VMEM),
        ],
        out_specs=(pl.BlockSpec(memory_space=pltpu.VMEM), pl.BlockSpec(memory_space=pltpu.VMEM)),
        scratch_shapes=[
            pltpu.VMEM((PIECES, 256, PIECE), jnp.bfloat16),
            pltpu.VMEM((DEPTH, max(WIDTHS)), jnp.int32),
            pltpu.SMEM((2,), jnp.int32),
            pltpu.SMEM((1,), jnp.int32),
            *[pltpu.VMEM((COLUMNS, w), jnp.bfloat16) for w in WIDTHS],
            *[pltpu.VMEM((8, 2, 16, w), jnp.float32) for w in WIDTHS],
            *[pltpu.VMEM((8, 16, w), jnp.float32) for w in WIDTHS],
            *[pltpu.VMEM((8, 16, w), jnp.float32) for w in WIDTHS],
            *[pltpu.VMEM((8, 16, w), jnp.float32) for w in WIDTHS],
            *[pltpu.VMEM((16, w), jnp.float32) for w in WIDTHS],
            *[pltpu.VMEM((8, 16, w), jnp.float32) for w in WIDTHS],
            *[pltpu.VMEM((16, w), jnp.bfloat16) for w in WIDTHS],
            dma((PIECES,)),
            dma((2,)),
            dma((CHUNKS,)),
            dma((CHUNKS,)),
            dma((CHUNKS, 8)),
            dma((CHUNKS, 8)),
            dma((CHUNKS, 8)),
            dma((CHUNKS, 8)),
        ],
        compiler_params=pltpu.CompilerParams(
            collective_id=0, has_side_effects=True, vmem_limit_bytes=24 << 20
        ),
        cost_estimate=pl.CostEstimate(
            flops=2 * 256 * COLUMNS * RANK, bytes_accessed=3 << 20, transcendentals=0
        ),
    )(gradient, seeds, adam_step.reshape(1, 1))
    new_first = 0.9 * first_moment + 0.1 * estimate
    new_second = 0.95 * second_moment + 0.05 * estimate * estimate
    corrected = jnp.sqrt(new_second * fix[4:5]) + 1e-08
    step_update = new_first * fix[0:1] / corrected
    return (new_first, new_second, step_update)


def solution(mesh):
    rows = P(("fsdp", "replica"), "tensor")
    return jax.shard_map(
        per_device,
        mesh=mesh,
        in_specs=(P("replica", "fsdp", "tensor"), P(), P(), rows, rows),
        out_specs=(rows, rows, rows),
        check_vma=False,
    )
```

time: 48.2 us -> 45.8 us (0.950)
  Pallas kernels: 45.7 us -> 43.3 us
    pallas_call x1, Pallas kernels: 45.7 us -> 43.3 us  [per_device(): pl.pallas_call(kernel, out_shape=(pltpu.VMEM((16, COLUMNS), jnp.float32),...]
where the time goes in v3:
time: 45.8 us; the launch traced here: 45.6 us
  Pallas kernels  43.3 us (95%)
  between operations  1.38 us (3%)
  other arithmetic  0.91 us (2%)
    pallas_call x1, Pallas kernels, per_device(): pl.pallas_call(kernel, out_shape=(pltpu.VMEM((16, COLUMNS), jnp.float32),...  43.3 us

profile of v3, /device:TPU:1, one launch (start us, length us, event | category | flops | bytes accessed | tf_op | source)
XLA Modules:
  0.0 45.6 jit_solution(11632987754797672123)
XLA Ops:
  0.6 0.0 copy-start
  0.6 0.0 copy-start.1
  1.3 43.3 %shard_map.76 = (f32[16,3584]{1,0:T(8,128)S(1)}, f32[8,3584]{1,0:T(8,128)S(1)}) custom-call(bf16[256,3584]{1,0:T(8,128)(2,1)} %bitcast.3, s32[2]{0:T(128)} %seeds_ref.1, s32[1,1]{1,0:T(1,128)} %bitcast.2.step_ref), custom_call_target="tpu_custom_call" | custom-call | flops 939524096 | bytes 3145728 | tf_op jit(solution)/shard_map/pallas_call | solution.py:272
  44.6 0.1 slice_reduce_fusion.1
  44.7 0.0 copy-done
  44.7 0.0 copy-done.1
  44.7 0.9 %add_divide_fusion = (f32[16,3584]{1,0:T(8,128)}, f32[16,3584]{1,0:T(8,128)}, f32[16,3584]{1,0:T(8,128)}) fusion(f32[3584]{0:T(1024)S(1)} %get-tuple-element.8, f32[3584]{0:T(1024)S(1)} %get-tuple-element.7, f32[16,3584]{1,0:T(8,128)S(1)} %get-tuple-element.5, f32[16,3584]{1,0:T(8,128)S(1)} %copy-done, f32[16,3584]{1,0:T(8,128)S(1)} %copy-done.1), kind=kLoop, calls=%fused_computation.2 | loop fusion | flops 630784 | bytes 1404928 | tf_op jit(solution)/shard_map/div | solution.py:313
Async XLA Ops:
  0.6 44.1 %copy-start = (f32[16,3584]{1,0:T(8,128)S(1)}, f32[16,3584]{1,0:T(8,128)}, u32[]{:S(2)}) copy-start(f32[16,3584]{1,0:T(8,128)} %param.9) | copy-start | bytes 688132
  0.6 44.1 %copy-start.1 = (f32[16,3584]{1,0:T(8,128)S(1)}, f32[16,3584]{1,0:T(8,128)}, u32[]{:S(2)}) copy-start(f32[16,3584]{1,0:T(8,128)} %param.8) | copy-start | bytes 688132

commit v4 on v3

--- a/solution.py
+++ b/solution.py
@@ -11,11 +11,10 @@
 COLUMNS = 3584
 WIDTHS = (384, 128)
 STARTS = (0, 384)
+WIRE = (jnp.float32, jnp.bfloat16)
 CHUNKS = len(WIDTHS)
 DEPTH = 512
 BLOCKS = COLUMNS // DEPTH
-PIECE = 896
-PIECES = COLUMNS // PIECE
 X_ORDER = (4, 3, 5, 2, 6, 1, 7)
 Z_ORDER = ((2, 0), (2, 1), (1, 0), (1, 1), (3, 0), (3, 1), (0, 1), (0, 0))
 WEYL = -1640531535
@@ -50,11 +49,11 @@
 
 
 def kernel(gradient_ref, seeds_ref, step_ref, out_ref, fix_ref, *scratch):
-    grad, base, seeds, when = scratch[:4]
-    per_chunk = [scratch[4 + i * CHUNKS : 4 + (i + 1) * CHUNKS] for i in range(7)]
+    grad, base, seeds = scratch[:3]
+    per_chunk = [scratch[3 + i * CHUNKS : 3 + (i + 1) * CHUNKS] for i in range(7)]
     proj, acc, got1, out2, got2, out3, got3 = per_chunk
-    sketch = scratch[4 + 7 * CHUNKS : 4 + 8 * CHUNKS]
-    grad_sem, small_sem, send1, recv1, send2, recv2, send3, recv3 = scratch[4 + 8 * CHUNKS :]
+    sketch = scratch[3 + 7 * CHUNKS : 3 + 8 * CHUNKS]
+    small_sem, send1, recv1, send2, recv2, send3, recv3 = scratch[3 + 8 * CHUNKS :]
     tensor = lax.axis_index("tensor")
     replica = lax.axis_index("replica")
     core = lax.rem(tensor, 2)
@@ -90,13 +89,8 @@
                 device_id_type=MESH,
             )
 
-    def grad_copy(piece):
-        return pltpu.make_async_copy(
-            gradient_ref.at[:, pl.ds(piece * PIECE, PIECE)], grad.at[piece], grad_sem.at[piece]
-        )
-
-    for piece in range(PIECES):
-        grad_copy(piece).start()
+    grad_copy = pltpu.make_async_copy(gradient_ref, grad, small_sem.at[1])
+    grad_copy.start()
 
     rows = lax.broadcasted_iota(jnp.int32, base.shape, 0)
     lanes = lax.broadcasted_iota(jnp.int32, base.shape, 1)
@@ -117,14 +111,7 @@
         lax.fori_loop(lower, upper, step, 0)
 
     def multiply(chunk):
-        part = None
-        for piece in range(PIECES):
-            term = jnp.dot(
-                grad[piece],
-                proj[chunk][piece * PIECE : (piece + 1) * PIECE, :],
-                preferred_element_type=jnp.float32,
-            )
-            part = term if part is None else part + term
+        part = jnp.dot(grad[...], proj[chunk][...], preferred_element_type=jnp.float32)
         acc[chunk][...] = part.reshape(8, 2, 16, WIDTHS[chunk])
 
     def copy1(chunk):
@@ -187,16 +174,16 @@
 
     def stage2(chunk):
         copy1(chunk).wait_recv()
-        out2[chunk][...] = acc[chunk][:, core] + got1[chunk][...]
+        out2[chunk][...] = (acc[chunk][:, core] + got1[chunk][...]).astype(WIRE[chunk])
         for step in X_ORDER:
             copy2(chunk, step).start()
 
     def stage3(chunk):
-        total = out2[chunk][x]
+        total = acc[chunk][x, core] + got1[chunk][x]
         for step in range(1, 8):
             arrive2(chunk, step).wait_recv()
-            total = total + got2[chunk][x_peer(step)]
-        out3[chunk][...] = total
+            total = total + got2[chunk][x_peer(step)].astype(jnp.float32)
+        out3[chunk][...] = total.astype(WIRE[chunk])
         for number in range(7):
             copy3(chunk, number).start()
 
@@ -215,14 +202,14 @@
             def _():
                 arrive3(chunk, far).wait_recv()
 
-        total = got3[chunk][0]
+        total = got3[chunk][0].astype(jnp.float32)
         for far in range(1, 8):
-            total = total + got3[chunk][far]
+            total = total + got3[chunk][far].astype(jnp.float32)
         sketch[chunk][...] = (total * (1.0 / 16)).astype(jnp.bfloat16)
 
     def back(chunk, first):
-        for piece in range(PIECES):
-            part = slice(piece * PIECE, (piece + 1) * PIECE)
+        for start in range(0, COLUMNS, DEPTH):
+            part = slice(start, start + DEPTH)
             term = lax.dot_general(
                 sketch[chunk][...],
                 proj[chunk][part, :],
@@ -232,8 +219,7 @@
             out_ref[:, part] = term if first else out_ref[:, part] + term
 
     generate(0, 0, BLOCKS)
-    for piece in range(PIECES):
-        grad_copy(piece).wait()
+    grad_copy.wait()
     multiply(0)
     pl.semaphore_wait(barrier, jnp.where(same, 15, 16))
     stage1(0)
@@ -279,19 +265,17 @@
         ],
         out_specs=(pl.BlockSpec(memory_space=pltpu.VMEM), pl.BlockSpec(memory_space=pltpu.VMEM)),
         scratch_shapes=[
-            pltpu.VMEM((PIECES, 256, PIECE), jnp.bfloat16),
+            pltpu.VMEM((256, COLUMNS), jnp.bfloat16),
             pltpu.VMEM((DEPTH, max(WIDTHS)), jnp.int32),
             pltpu.SMEM((2,), jnp.int32),
-            pltpu.SMEM((1,), jnp.int32),
             *[pltpu.VMEM((COLUMNS, w), jnp.bfloat16) for w in WIDTHS],
             *[pltpu.VMEM((8, 2, 16, w), jnp.float32) for w in WIDTHS],
             *[pltpu.VMEM((8, 16, w), jnp.float32) for w in WIDTHS],
-            *[pltpu.VMEM((8, 16, w), jnp.float32) for w in WIDTHS],
-            *[pltpu.VMEM((8, 16, w), jnp.float32) for w in WIDTHS],
-            *[pltpu.VMEM((16, w), jnp.float32) for w in WIDTHS],
-            *[pltpu.VMEM((8, 16, w), jnp.float32) for w in WIDTHS],
+            *[pltpu.VMEM((8, 16, w), t) for w, t in zip(WIDTHS, WIRE)],
+            *[pltpu.VMEM((8, 16, w), t) for w, t in zip(WIDTHS, WIRE)],
+            *[pltpu.VMEM((16, w), t) for w, t in zip(WIDTHS, WIRE)],
+            *[pltpu.VMEM((8, 16, w), t) for w, t in zip(WIDTHS, WIRE)],
             *[pltpu.VMEM((16, w), jnp.bfloat16) for w in WIDTHS],
-            dma((PIECES,)),
             dma((2,)),
             dma((CHUNKS,)),
             dma((CHUNKS,)),

time: 45.8 us -> 44.9 us (0.980)
  Pallas kernels: 43.3 us -> 42.4 us
    pallas_call x1, Pallas kernels: 43.3 us -> 42.4 us  [per_device(): pl.pallas_call(kernel, out_shape=(pltpu.VMEM((16, COLUMNS), jnp.float32),...]
where the time goes in v4:
time: 44.9 us; the launch traced here: 44.7 us
  Pallas kernels  42.4 us (94%)
  between operations  1.38 us (3%)
  other arithmetic  0.91 us (2%)
    pallas_call x1, Pallas kernels, per_device(): pl.pallas_call(kernel, out_shape=(pltpu.VMEM((16, COLUMNS), jnp.float32),...  42.4 us
    div x1, other arithmetic, per_device(): step_update = new_first * fix[0:1] / corrected  0.91 us

profile of v4, /device:TPU:1, one launch (start us, length us, event | category | flops | bytes accessed | tf_op | source)
XLA Modules:
  0.0 44.7 jit_solution(8918940591882236227)
XLA Ops:
  0.6 0.0 copy-start
  0.6 0.0 copy-start.1
  1.3 42.4 %shard_map.76 = (f32[16,3584]{1,0:T(8,128)S(1)}, f32[8,3584]{1,0:T(8,128)S(1)}) custom-call(bf16[256,3584]{1,0:T(8,128)(2,1)} %bitcast.3, s32[2]{0:T(128)} %seeds_ref.1, s32[1,1]{1,0:T(1,128)} %bitcast.2.step_ref), custom_call_target="tpu_custom_call" | custom-call | flops 939524096 | bytes 3145728 | tf_op jit(solution)/shard_map/pallas_call | solution.py:258
  43.7 0.1 slice_reduce_fusion.1
  43.8 0.0 copy-done
  43.8 0.0 copy-done.1
  43.8 0.9 %add_divide_fusion = (f32[16,3584]{1,0:T(8,128)}, f32[16,3584]{1,0:T(8,128)}, f32[16,3584]{1,0:T(8,128)}) fusion(f32[3584]{0:T(1024)S(1)} %get-tuple-element.8, f32[3584]{0:T(1024)S(1)} %get-tuple-element.7, f32[16,3584]{1,0:T(8,128)S(1)} %get-tuple-element.5, f32[16,3584]{1,0:T(8,128)S(1)} %copy-done, f32[16,3584]{1,0:T(8,128)S(1)} %copy-done.1), kind=kLoop, calls=%fused_computation.2 | loop fusion | flops 630784 | bytes 1404928 | tf_op jit(solution)/shard_map/div | solution.py:297
Async XLA Ops:
  0.6 43.2 %copy-start = (f32[16,3584]{1,0:T(8,128)S(1)}, f32[16,3584]{1,0:T(8,128)}, u32[]{:S(2)}) copy-start(f32[16,3584]{1,0:T(8,128)} %param.9) | copy-start | bytes 688132
  0.6 43.2 %copy-start.1 = (f32[16,3584]{1,0:T(8,128)S(1)}, f32[16,3584]{1,0:T(8,128)}, u32[]{:S(2)}) copy-start(f32[16,3584]{1,0:T(8,128)} %param.8) | copy-start | bytes 688132

commit v5 on v4

--- a/solution.py
+++ b/solution.py
@@ -13,13 +13,15 @@
 STARTS = (0, 384)
 WIRE = (jnp.float32, jnp.bfloat16)
 CHUNKS = len(WIDTHS)
-DEPTH = 512
+DEPTH = 896
 BLOCKS = COLUMNS // DEPTH
 X_ORDER = (4, 3, 5, 2, 6, 1, 7)
 Z_ORDER = ((2, 0), (2, 1), (1, 0), (1, 1), (3, 0), (3, 1), (0, 1), (0, 0))
 WEYL = -1640531535
 MESH = pl.DeviceIdType.MESH
 SINE = (6.28317941 / 16, -41.33894249 / 16, 81.39535834 / 16, -71.47469135 / 16)
+SCALE = -((-SINE[3]) ** (1.0 / 7.0))
+MONIC = tuple(SINE[k] / SCALE ** (2 * k + 1) for k in range(3))
 
 
 def srl(value, bits):
@@ -40,12 +42,11 @@
     negative_log = 16.635532333438686 - jnp.log(srl(hash_a, 8).astype(jnp.float32) + 0.5)
     radius = negative_log * lax.rsqrt(jnp.maximum(negative_log, 1e-30))
     turn = lax.shift_right_arithmetic(hash_b, jnp.full_like(hash_b, 8)).astype(jnp.float32) + 0.5
-    z = 0.25 - jnp.abs(turn) * (1.0 / 16777216.0)
-    square = z * z
-    poly = SINE[3] * square + SINE[2]
-    poly = poly * square + SINE[1]
-    poly = poly * square + SINE[0]
-    return (poly * z) * radius
+    y = SCALE / 4 - jnp.abs(turn) * (SCALE / 16777216.0)
+    square = y * y
+    poly = (square + MONIC[2]) * square + MONIC[1]
+    poly = poly * square + MONIC[0]
+    return (poly * y) * radius
 
 
 def kernel(gradient_ref, seeds_ref, step_ref, out_ref, fix_ref, *scratch):
@@ -223,9 +224,9 @@
     multiply(0)
     pl.semaphore_wait(barrier, jnp.where(same, 15, 16))
     stage1(0)
-    generate(1, 0, 4)
+    generate(1, 0, 2)
     stage2(0)
-    generate(1, 4, BLOCKS)
+    generate(1, 2, BLOCKS)
     multiply(1)
     stage1(1)
     stage2(1)

time: 44.9 us -> 44.7 us (level)
  no operation moved by 1% of the time
where the time goes in v5:
time: 44.7 us; the launch traced here: 44.5 us
  Pallas kernels  42.2 us (94%)
  between operations  1.38 us (3%)
  other arithmetic  0.91 us (2%)
    pallas_call x1, Pallas kernels, per_device(): pl.pallas_call(kernel, out_shape=(pltpu.VMEM((16, COLUMNS), jnp.float32),...  42.2 us
    div x1, other arithmetic, per_device(): step_update = new_first * fix[0:1] / corrected  0.91 us

profile of v5, /device:TPU:1, one launch (start us, length us, event | category | flops | bytes accessed | tf_op | source)
XLA Modules:
  0.0 44.5 jit_solution(15284630668645774567)
XLA Ops:
  0.6 0.0 copy-start
  0.6 0.0 copy-start.1
  1.3 42.2 %shard_map.76 = (f32[16,3584]{1,0:T(8,128)S(1)}, f32[8,3584]{1,0:T(8,128)S(1)}) custom-call(bf16[256,3584]{1,0:T(8,128)(2,1)} %bitcast.3, s32[2]{0:T(128)} %seeds_ref.1, s32[1,1]{1,0:T(1,128)} %bitcast.2.step_ref), custom_call_target="tpu_custom_call" | custom-call | flops 939524096 | bytes 3145728 | tf_op jit(solution)/shard_map/pallas_call | solution.py:259
  43.5 0.1 slice_reduce_fusion.1
  43.6 0.0 copy-done
  43.6 0.0 copy-done.1
  43.6 0.9 %add_divide_fusion = (f32[16,3584]{1,0:T(8,128)}, f32[16,3584]{1,0:T(8,128)}, f32[16,3584]{1,0:T(8,128)}) fusion(f32[3584]{0:T(1024)S(1)} %get-tuple-element.8, f32[3584]{0:T(1024)S(1)} %get-tuple-element.7, f32[16,3584]{1,0:T(8,128)S(1)} %get-tuple-element.5, f32[16,3584]{1,0:T(8,128)S(1)} %copy-done, f32[16,3584]{1,0:T(8,128)S(1)} %copy-done.1), kind=kLoop, calls=%fused_computation.2 | loop fusion | flops 630784 | bytes 1404928 | tf_op jit(solution)/shard_map/div | solution.py:298
Async XLA Ops:
  0.6 43.0 %copy-start = (f32[16,3584]{1,0:T(8,128)S(1)}, f32[16,3584]{1,0:T(8,128)}, u32[]{:S(2)}) copy-start(f32[16,3584]{1,0:T(8,128)} %param.9) | copy-start | bytes 688132
  0.6 43.0 %copy-start.1 = (f32[16,3584]{1,0:T(8,128)S(1)}, f32[16,3584]{1,0:T(8,128)}, u32[]{:S(2)}) copy-start(f32[16,3584]{1,0:T(8,128)} %param.8) | copy-start | bytes 688132
